TPU v7x, 32 devices: a whole 2x2x4 slice. The times are simulated.
32 devices in a mesh: dp: 8 (over y, x, core), tensor: 4 (over z).
Axes of the slice: x: 2, y: 2, z: 4, core: 2. Of those that a mesh axis runs over, the one named last changes fastest.
Arguments:
- tokens: bfloat16 [16384, 1024], P(('dp', 'tensor')), may hold values from -16 to 16
- prompts: bfloat16 [8, 64, 1024], P('dp'), may hold values from -6 to 6
- w_attn: bfloat16 [3, 1024, 1024], P(None, None, 'tensor'), may hold values from -0.1875 to 0.1875
- w_out: bfloat16 [1024, 1024], P('tensor'), may hold values from -0.1875 to 0.1875
- norm_gain: float32 [2, 1024], replicated, may hold values from 0.1 to 1.9
- norm_bias: float32 [2, 1024], replicated, may hold values from -3 to 3
- w_in: bfloat16 [1024, 4096], P(None, 'tensor'), may hold values from -0.1875 to 0.1875
- b_in: float32 [4096], P('tensor'), may hold values from -3 to 3
- w_down: bfloat16 [4096, 1024], P('tensor'), may hold values from -0.09375 to 0.09375
- index_rows: bfloat16 [16384, 1024], P('dp'), may hold values from -6 to 6
- lengths: int32 [8, 32], P('dp'), may hold values from 1 to 512, 2048 in all within a row
- groups: int32 [256], P('dp'), may hold values from 0 to 7
- candidates: int32 [256, 64], P(('dp', 'tensor')), may hold values from 0 to 16383
Outputs:
- scores: float32 [256, 64], P(('dp', 'tensor'))
All inputs are finite; a program needn't handle non-finite values.
Results may differ from a plain program's by a relative error of at most 0.01.
Values may be sent and summed in bfloat16 or wider, within the bound.
A program may use at most 128 MiB of HBM per device.

v0:
```python
import jax
import jax.numpy as jnp
from jax import lax
from jax.sharding import PartitionSpec as P

D = 1024
HEAD_DIM = 64


def layer_norm(values, gain, bias):
    mean = jnp.mean(values, axis=-1, keepdims=True)
    centred = values - mean
    var = jnp.mean(centred * centred, axis=-1, keepdims=True)
    return centred * lax.rsqrt(var + 1e-05) * gain + bias


def project(block, weight):
    return jnp.dot(block, weight, preferred_element_type=jnp.float32).astype(jnp.bfloat16)


def shards(
    tokens,
    prompts,
    w_attn,
    w_out,
    norm_gain,
    norm_bias,
    w_in,
    b_in,
    w_down,
    index_rows,
    lengths,
    groups,
    candidates,
):
    shard_rows = tokens.shape[0]
    tok_dev = shard_rows * lax.axis_size("tensor")
    columns = w_attn.shape[2]
    heads_here = columns // HEAD_DIM
    scale = HEAD_DIM ** (-0.5)
    whole = lax.all_gather(tokens, "tensor", axis=0, tiled=True)
    query = (jnp.dot(whole, w_attn[0], preferred_element_type=jnp.float32) * scale).astype(
        jnp.bfloat16
    )
    keys = project(whole, w_attn[1])
    values = project(whole, w_attn[2])
    every_prompt = lax.all_gather(prompts, "dp", axis=0, tiled=True)
    flat = every_prompt.reshape(-1, every_prompt.shape[2])
    prompt_key = project(flat, w_attn[1])
    prompt_value = project(flat, w_attn[2])
    prompt_len = prompts.shape[1]
    prompt_rows = prompt_key.shape[0]
    lens = lengths[0]
    texts_here = lens.shape[0]
    text_ids = jnp.arange(texts_here, dtype=jnp.int32)
    ends = jnp.sum(jnp.where(text_ids[None, :] <= text_ids[:, None], lens[None, :], 0), axis=1)
    position = jnp.arange(tok_dev, dtype=jnp.int32)
    seg = jnp.sum((position[:, None] >= ends[None, :]).astype(jnp.int32), axis=1)
    tok_group = jnp.sum(jnp.where(seg[:, None] == text_ids[None, :], groups[None, :], 0), axis=1)
    key_group = jnp.arange(prompt_rows, dtype=jnp.int32) // prompt_len
    all_keys = jnp.concatenate([keys, prompt_key], axis=0).reshape(-1, heads_here, HEAD_DIM)
    all_values = jnp.concatenate([values, prompt_value], axis=0).reshape(-1, heads_here, HEAD_DIM)
    block = min(512, tok_dev)

    def attend(number):
        start = number * block
        q_block = lax.dynamic_slice_in_dim(query, start, block, 0).reshape(
            block, heads_here, HEAD_DIM
        )
        seg_block = lax.dynamic_slice_in_dim(seg, start, block, 0)
        group_block = lax.dynamic_slice_in_dim(tok_group, start, block, 0)
        allowed = jnp.concatenate(
            [seg_block[:, None] == seg[None, :], group_block[:, None] == key_group[None, :]], axis=1
        )
        logits = jnp.einsum("qhe,khe->hqk", q_block, all_keys, preferred_element_type=jnp.float32)
        logits = jnp.where(allowed[None], logits, jnp.float32(-1e30))
        top = jnp.max(logits, axis=2, keepdims=True)
        weights = jnp.exp(logits - top)
        total = jnp.sum(weights, axis=2, keepdims=True)
        probs = (weights / total).astype(jnp.bfloat16)
        mixed = jnp.einsum("hqk,khe->qhe", probs, all_values, preferred_element_type=jnp.float32)
        return mixed.astype(jnp.bfloat16).reshape(block, columns)

    context = lax.map(attend, jnp.arange(tok_dev // block, dtype=jnp.int32)).reshape(
        tok_dev, columns
    )
    my_start = lax.axis_index("tensor") * shard_rows
    attn_part = lax.psum_scatter(
        jnp.dot(context, w_out, preferred_element_type=jnp.float32),
        "tensor",
        scatter_dimension=0,
        tiled=True,
    )
    normed_rows = layer_norm(
        tokens.astype(jnp.float32) + attn_part, norm_gain[0], norm_bias[0]
    ).astype(jnp.bfloat16)
    expanded = jax.nn.gelu(
        jnp.dot(
            lax.all_gather(normed_rows, "tensor", axis=0, tiled=True),
            w_in,
            preferred_element_type=jnp.float32,
        )
        + b_in,
        approximate=False,
    ).astype(jnp.bfloat16)
    reduced = lax.psum_scatter(
        jnp.dot(expanded, w_down, preferred_element_type=jnp.float32).astype(jnp.bfloat16),
        "tensor",
        scatter_dimension=0,
        tiled=True,
    ).astype(jnp.float32)
    output = layer_norm(
        normed_rows.astype(jnp.float32) + reduced, norm_gain[1], norm_bias[1]
    ).astype(jnp.bfloat16)
    seg_rows = lax.dynamic_slice_in_dim(seg, my_start, shard_rows, 0)
    member = (text_ids[:, None] == seg_rows[None, :]).astype(jnp.bfloat16)
    partial_sums = jnp.dot(member, output, preferred_element_type=jnp.float32)
    pooled_sums = lax.psum_scatter(partial_sums, "tensor", scatter_dimension=0, tiled=True)
    mine = pooled_sums.shape[0]
    my_lens = lax.dynamic_slice_in_dim(lens, lax.axis_index("tensor") * mine, mine, 0)
    pooled = pooled_sums / my_lens[:, None].astype(jnp.float32)
    square = jnp.mean(pooled * pooled, axis=1, keepdims=True)
    embedding = (pooled * lax.rsqrt(square + 1e-06)).astype(jnp.bfloat16)
    asked_vectors, asked_rows = (
        lax.all_gather(embedding, "dp", axis=0, tiled=True),
        lax.all_gather(candidates, "dp", axis=0, tiled=True),
    )
    held = index_rows.shape[0]
    local_rows = asked_rows - lax.axis_index("dp") * held
    owned = (local_rows >= 0) & (local_rows < held)
    table = jnp.dot(asked_vectors, index_rows.T, preferred_element_type=jnp.float32) * D ** (-0.5)
    picked = jnp.take_along_axis(table, jnp.clip(local_rows, 0, held - 1), axis=1)
    picked = jnp.where(owned, picked, jnp.float32(0.0))
    return lax.psum_scatter(
        picked.astype(jnp.bfloat16), "dp", scatter_dimension=0, tiled=True
    ).astype(jnp.float32)


def solution(mesh):
    placed = (
        P(("dp", "tensor"), None),
        P("dp", None, None),
        P(None, None, "tensor"),
        P("tensor", None),
        P(),
        P(),
        P(None, "tensor"),
        P("tensor"),
        P("tensor", None),
        P("dp", None),
        P("dp", None),
        P("dp"),
        P(("dp", "tensor"), None),
    )
    return jax.shard_map(
        shards, mesh=mesh, in_specs=placed, out_specs=P(("dp", "tensor"), None), check_vma=False
    )
```

profile of v0, /device:TPU:0, one launch (start us, length us, event | category | flops | bytes accessed | tf_op | source)
XLA Modules:
  0.0 692.5 jit_solution(8815590890607016077)
XLA Ops:
  6.5 0.7 all-gather.6.cloned.1.call-update
  7.3 0.7 all-gather.4.cloned.1.call-update
  8.1 0.8 select_reduce_fusion.2
  9.0 0.8 select_reduce_fusion.1
  9.7 25.7 %all-gather.6.cloned.1.call-done = bf16[8,64,1024]{2,1,0:T(8,128)(2,1)} async-done(((bf16[1,64,1024]{2,1,0:T(8,128)(2,1)}), bf16[8,64,1024]{2,1,0:T(8,128)(2,1)}) %all-gather.6.cloned.1.call-update) | async-done | bytes 1048592 | tf_op jit(solution)/shard_map/all_gather | solution.py:47
  35.5 2.5 convolution_convert_fusion.3
  38.0 2.5 convolution_convert_fusion.2
  40.5 77.3 %all-gather.4.cloned.1.call-done = bf16[2048,1024]{1,0:T(8,128)(2,1)} async-done(((bf16[512,1024]{1,0:T(8,128)(2,1)}), bf16[2048,1024]{1,0:T(8,128)(2,1)}) %all-gather.4.cloned.1.call-update) | async-done | bytes 4194320 | tf_op jit(solution)/shard_map/all_gather | solution.py:41
  117.8 3.6 convolution_convert_fusion.1
  121.5 1.8 copy.25
  123.3 3.6 convolution_convert_fusion
  127.0 1.6 copy.26
  128.6 4.5 fusion.33
  133.2 114.9 %while.11 = (s32[]{:T(128)}, bf16[4,512,256]{2,1,0:T(8,128)(2,1)}, s32[4]{0:T(128)S(1)}, s32[2048]{0:T(1024)S(1)}, s32[2048]{0:T(1024)S(1)}, /*index=5*/bf16[204...) while((s32[]{:T(128)}, bf16[4,512,256]{2,1,0:T(8,128)(2,1)}, ...), condition=%wide.region_6.7_spmd.clone, body=%wide.region_3.6_spmd.clone.sunk | while | flops 1371150848 | bytes 52470456 | solution.py:84
  133.2 0.7 dynamic_slice.32
  134.6 0.7 broadcast_compare_fusion.5
  135.7 1.7 constant_dynamic-slice_fusion.2
  137.3 1.8 copy.34
  139.2 12.7 %fusion.108 = (f32[4,512]{1,0:T(4,128)S(1)}, f32[4,512,2560]{2,1,0:T(8,128)}) fusion(pred[512,2560]{1,0:T(8,128)(4,1)S(1)} %pad_add_fusion.2, bf16[512,4,64]{0,2,1:T(8,128)(2,1)} %bitcast.63, bf16[2560,4,64]{0,2,1:T(8,128)(2,1)} %get-tuple-element.208), kind=kOutput, calls=%fused_computation.127.clone.1 | convolution fusion | flops 686819840 | bytes 23863296 | tf_op jit(solution)/shard_map/while/body/eval_jaxpr/sub | solution.py:78
  151.9 9.1 %fusion.109 = bf16[4,512,64]{1,2,0:T(8,128)(2,1)S(1)} fusion(bf16[2560,4,64]{0,2,1:T(8,128)(2,1)} %get-tuple-element.209, f32[4,512,2560]{2,1,0:T(8,128)} %get-tuple-element.176, f32[4,512]{1,0:T(4,128)S(1)} %get-tuple-element.177), kind=kOutput, calls=%fused_computation.13.clone.1 | convolution fusion | flops 681705472 | bytes 22552576 | tf_op jit(solution)/shard_map/while/body/eval_jaxpr/hqk,khe->qhe/dot_general | solution.py:81
  161.2 0.7 constant_dynamic-update-slice_fusion.2
  161.9 0.7 dynamic_slice.32
  163.3 0.7 broadcast_compare_fusion.5
  164.4 1.7 constant_dynamic-slice_fusion.2
  166.1 1.8 copy.34
  167.9 12.7 %fusion.108 = (f32[4,512]{1,0:T(4,128)S(1)}, f32[4,512,2560]{2,1,0:T(8,128)}) fusion(pred[512,2560]{1,0:T(8,128)(4,1)S(1)} %pad_add_fusion.2, bf16[512,4,64]{0,2,1:T(8,128)(2,1)} %bitcast.63, bf16[2560,4,64]{0,2,1:T(8,128)(2,1)} %get-tuple-element.208), kind=kOutput, calls=%fused_computation.127.clone.1 | convolution fusion | flops 686819840 | bytes 23863296 | tf_op jit(solution)/shard_map/while/body/eval_jaxpr/sub | solution.py:78
  180.6 9.1 %fusion.109 = bf16[4,512,64]{1,2,0:T(8,128)(2,1)S(1)} fusion(bf16[2560,4,64]{0,2,1:T(8,128)(2,1)} %get-tuple-element.209, f32[4,512,2560]{2,1,0:T(8,128)} %get-tuple-element.176, f32[4,512]{1,0:T(4,128)S(1)} %get-tuple-element.177), kind=kOutput, calls=%fused_computation.13.clone.1 | convolution fusion | flops 681705472 | bytes 22552576 | tf_op jit(solution)/shard_map/while/body/eval_jaxpr/hqk,khe->qhe/dot_general | solution.py:81
  189.9 0.7 constant_dynamic-update-slice_fusion.2
  190.6 0.7 dynamic_slice.32
  192.1 0.7 broadcast_compare_fusion.5
  193.1 1.7 constant_dynamic-slice_fusion.2
  194.8 1.8 copy.34
  196.6 12.7 %fusion.108 = (f32[4,512]{1,0:T(4,128)S(1)}, f32[4,512,2560]{2,1,0:T(8,128)}) fusion(pred[512,2560]{1,0:T(8,128)(4,1)S(1)} %pad_add_fusion.2, bf16[512,4,64]{0,2,1:T(8,128)(2,1)} %bitcast.63, bf16[2560,4,64]{0,2,1:T(8,128)(2,1)} %get-tuple-element.208), kind=kOutput, calls=%fused_computation.127.clone.1 | convolution fusion | flops 686819840 | bytes 23863296 | tf_op jit(solution)/shard_map/while/body/eval_jaxpr/sub | solution.py:78
  209.3 9.1 %fusion.109 = bf16[4,512,64]{1,2,0:T(8,128)(2,1)S(1)} fusion(bf16[2560,4,64]{0,2,1:T(8,128)(2,1)} %get-tuple-element.209, f32[4,512,2560]{2,1,0:T(8,128)} %get-tuple-element.176, f32[4,512]{1,0:T(4,128)S(1)} %get-tuple-element.177), kind=kOutput, calls=%fused_computation.13.clone.1 | convolution fusion | flops 681705472 | bytes 22552576 | tf_op jit(solution)/shard_map/while/body/eval_jaxpr/hqk,khe->qhe/dot_general | solution.py:81
  218.6 0.7 constant_dynamic-update-slice_fusion.2
  219.4 0.7 dynamic_slice.32
  220.8 0.7 broadcast_compare_fusion.5
  221.9 1.7 constant_dynamic-slice_fusion.2
  223.5 1.8 copy.34
  225.3 12.7 %fusion.108 = (f32[4,512]{1,0:T(4,128)S(1)}, f32[4,512,2560]{2,1,0:T(8,128)}) fusion(pred[512,2560]{1,0:T(8,128)(4,1)S(1)} %pad_add_fusion.2, bf16[512,4,64]{0,2,1:T(8,128)(2,1)} %bitcast.63, bf16[2560,4,64]{0,2,1:T(8,128)(2,1)} %get-tuple-element.208), kind=kOutput, calls=%fused_computation.127.clone.1 | convolution fusion | flops 686819840 | bytes 23863296 | tf_op jit(solution)/shard_map/while/body/eval_jaxpr/sub | solution.py:78
  238.1 9.1 %fusion.109 = bf16[4,512,64]{1,2,0:T(8,128)(2,1)S(1)} fusion(bf16[2560,4,64]{0,2,1:T(8,128)(2,1)} %get-tuple-element.209, f32[4,512,2560]{2,1,0:T(8,128)} %get-tuple-element.176, f32[4,512]{1,0:T(4,128)S(1)} %get-tuple-element.177), kind=kOutput, calls=%fused_computation.13.clone.1 | convolution fusion | flops 681705472 | bytes 22552576 | tf_op jit(solution)/shard_map/while/body/eval_jaxpr/hqk,khe->qhe/dot_general | solution.py:81
  247.4 0.7 constant_dynamic-update-slice_fusion.2
  248.1 5.8 fusion.82
  254.0 0.6 copy-done.7
  254.6 142.5 %reduce-scatter.4.cloned.1.call-done = f32[512,1024]{1,0:T(8,128)} async-done(((f32[2048,1024]{1,0:T(8,128)}), f32[512,1024]{1,0:T(8,128)}) %reduce-scatter.4.cloned.1.call-update) | async-done | bytes 2097168 | tf_op jit(solution)/shard_map/reduce_scatter | solution.py:88
  397.1 2.0 fusion.37
  399.8 1.6 add_convert_fusion.1
  401.7 81.4 %all-gather.8.cloned.1.call-done = bf16[2048,1024]{1,0:T(8,128)(2,1)} async-done(((bf16[512,1024]{1,0:T(8,128)(2,1)}), bf16[2048,1024]{1,0:T(8,128)(2,1)}) %all-gather.8.cloned.1.call-update) | async-done | bytes 4194320 | tf_op jit(solution)/shard_map/all_gather | solution.py:99
  483.1 28.5 %fusion.28 = bf16[2048,1024]{1,0:T(8,128)(2,1)} fusion(bf16[1024,1024]{1,0:T(8,128)(2,1)S(1)} %copy-done, f32[1024]{0:T(1024)S(1)} %copy-done.10, bf16[2048,1024]{1,0:T(8,128)(2,1)} %all-gather.8.cloned.1.call-done, bf16[1024,1024]{1,0:T(8,128)(2,1)} %param.21), kind=kOutput, calls=%fused_computation.45 | convolution fusion | flops 8730443776 | bytes 12587008 | tf_op jit(solution)/shard_map/dot_general | solution.py:107
  511.8 0.5 copy-done.9
  512.3 9.3 %all_gather.15 = s32[64,64]{1,0:T(8,128)S(1)} all-gather(s32[8,64]{1,0:T(8,128)S(1)} %copy-done.9), channel_id=1, replica_groups=mesh['dp'=8,'tensor'=4] {'dp'}, dimensions={0}, use_global_device_ids=true | all-gather | bytes 18432 | tf_op jit(solution)/shard_map/all_gather | solution.py:126
  521.6 65.5 %reduce-scatter.6.cloned.1.call-done = bf16[512,1024]{1,0:T(8,128)(2,1)} async-done(((bf16[2048,1024]{1,0:T(8,128)(2,1)}), bf16[512,1024]{1,0:T(8,128)(2,1)}) %reduce-scatter.6.cloned.1.call-update) | async-done | bytes 1048592 | tf_op jit(solution)/shard_map/reduce_scatter | solution.py:106
  587.1 1.7 fusion.35
  588.8 1.7 multiply_reduce_fusion
  590.5 1.3 fusion.36
  592.0 0.6 dynamic-slice.1
  593.3 18.5 %reduce-scatter.8.cloned.1.call-done = f32[8,1024]{1,0:T(8,128)} async-done(((f32[32,1024]{1,0:T(8,128)}), f32[8,1024]{1,0:T(8,128)}) %reduce-scatter.8.cloned.1.call-update) | async-done | bytes 32784 | tf_op jit(solution)/shard_map/reduce_scatter | solution.py:118
  611.8 0.9 multiply_reduce_fusion.2
  612.7 0.8 multiply_convert_fusion
  613.6 9.1 %all_gather.19 = bf16[64,1024]{1,0:T(8,128)(2,1)S(1)} all-gather(bf16[8,1024]{1,0:T(8,128)(2,1)S(1)} %multiply_convert_fusion), channel_id=1, replica_groups=mesh['dp'=8,'tensor'=4] {'dp'}, dimensions={0}, use_global_device_ids=true | all-gather | bytes 147456 | tf_op jit(solution)/shard_map/all_gather | solution.py:125
  622.6 3.6 convolution_multiply_fusion.1
  626.2 35.1 %gather_fusion = bf16[4096]{0:T(1024)(128)(2,1)S(1)} fusion(bf16[64,2048]{1,0:T(8,128)(2,1)S(1)} %convolution_multiply_fusion.1, s32[4096]{0:T(1024)S(1)} %reshape.87), kind=kCustom, calls=%fused_computation | custom fusion | bytes 49152 | tf_op jit(solution)/shard_map/jit(take_along_axis)/gather | solution.py:132
  661.5 23.6 %all-reduce = bf16[64,64]{1,0:T(8,128)(2,1)S(1)} all-reduce(bf16[64,64]{1,0:T(8,128)(2,1)S(1)} %select_convert_fusion), channel_id=5, replica_groups=mesh['dp'=8,'tensor'=4] {'dp'}, use_global_device_ids=true, to_apply=%region_15.16.clone | all-reduce | flops 4096 | bytes 16384
  685.0 0.6 dynamic-slice_convert_fusion
  (77 shorter events, 4.3 us)
Async XLA Ops:
  6.5 476.6 %copy-start = (bf16[1024,1024]{1,0:T(8,128)(2,1)S(1)}, bf16[1024,1024]{1,0:T(8,128)(2,1)}, u32[]{:S(2)}) copy-start(bf16[1024,1024]{1,0:T(8,128)(2,1)} %param.23) | copy-start | bytes 6291460
  6.5 28.9 %all-gather.6.cloned.1.call-start = ((), (), s32[]{:S(2)}) async-start(), calls=%async_computation.4 | async-start | bytes 1179648 | tf_op jit(solution)/shard_map/all_gather | solution.py:47
  7.3 110.6 %all-gather.4.cloned.1.call-start = ((), (), s32[]{:S(2)}) async-start(), calls=%async_computation.3 | async-start | bytes 5242880 | tf_op jit(solution)/shard_map/all_gather | solution.py:41
  8.0 389.1 %reduce-scatter.4.cloned.1.call-start = ((), (), s32[]{:S(2)}) async-start(), calls=%async_computation.5 | async-start | bytes 10485760 | tf_op jit(solution)/shard_map/reduce_scatter | solution.py:88
  117.8 3.6 copy-start.6
  123.3 3.6 copy-start.5
  253.9 0.7 copy-start.7
  253.9 0.7 copy-start.8
  253.9 143.2 %copy-start.3 = (bf16[512,1024]{1,0:T(8,128)(2,1)S(1)}, bf16[512,1024]{1,0:T(8,128)(2,1)}, u32[]{:S(2)}) copy-start(bf16[512,1024]{1,0:T(8,128)(2,1)} %param.15) | copy-start | bytes 3145732
  253.9 229.1 %all-gather.8.cloned.1.call-start = ((), (), s32[]{:S(2)}) async-start(), calls=%async_computation.6 | async-start | bytes 5242880 | tf_op jit(solution)/shard_map/all_gather | solution.py:99
  397.1 2.2 copy-start.1
  399.3 83.8 %copy-start.10 = (f32[1024]{0:T(1024)S(1)}, f32[1024]{0:T(1024)}, u32[]{:S(2)}) copy-start(f32[1024]{0:T(1024)} %param.22) | copy-start | bytes 12292
  401.4 185.6 %reduce-scatter.6.cloned.1.call-start = ((), (), s32[]{:S(2)}) async-start(), calls=%async_computation.7 | async-start | bytes 5242880 | tf_op jit(solution)/shard_map/reduce_scatter | solution.py:106
  511.6 0.7 copy-start.9
  511.6 75.5 %copy-start.2 = (bf16[512,1024]{1,0:T(8,128)(2,1)S(1)}, bf16[512,1024]{1,0:T(8,128)(2,1)}, u32[]{:S(2)}) copy-start(bf16[512,1024]{1,0:T(8,128)(2,1)} %add_convert_fusion.1) | copy-start | bytes 3145732
  511.7 80.3 %copy-start.12 = (u32[32]{0:T(128)S(1)}, u32[32]{0:T(128)}, u32[]{:S(2)}) copy-start(u32[32]{0:T(128)} %constant.170) | copy-start | bytes 388
  511.7 81.5 %copy-start.11 = (s32[1,32]{1,0:T(1,128)S(1)}, s32[1,32]{1,0:T(1,128)}, u32[]{:S(2)}) copy-start(s32[1,32]{1,0:T(1,128)} %param.25) | copy-start | bytes 388
  511.7 100.1 %reduce-scatter.8.cloned.1.call-start = ((), (), s32[]{:S(2)}) async-start(), calls=%async_computation.8 | async-start | bytes 163840 | tf_op jit(solution)/shard_map/reduce_scatter | solution.py:118
  587.1 3.4 copy-start.4
Sparse Core Ops, SparseCore 0:
  9.2 26.1 all-gather.5
  37.0 80.7 all-gather.3
  254.1 143.0 reduce-scatter.3
  401.6 81.4 all-gather.7
  511.8 75.2 reduce-scatter.5
  592.0 19.7 reduce-scatter.7
where the time goes:
time: 693 us; the launch traced here: 692 us
  waiting for transfers between devices  412 us (59%)
  matrix products  143 us (21%)
  local copies, waits for them, and re-layouts  61.3 us (9%)
  blocking collectives  42 us (6%)
  other arithmetic  15.7 us (2%)
  between operations  14.3 us (2%)
    reduce_scatter x1, waiting for transfers between devices, shards(): lax.psum_scatter(jnp.dot(context, w_out, preferred_element_type=jnp.float...  142 us
    all_gather x1, waiting for transfers between devices, shards(): lax.all_gather(normed_rows, 'tensor', axis=0, tiled=True)  81.4 us
    all_gather x1, waiting for transfers between devices, shards(): whole = lax.all_gather(tokens, 'tensor', axis=0, tiled=True)  77.3 us
    reduce_scatter x1, waiting for transfers between devices, shards(): lax.psum_scatter(jnp.dot(expanded, w_down, preferred_element_type=jnp.flo...  65.5 us
    sub x4, matrix products, attend(): weights = jnp.exp(logits - top)  50.9 us
    dot_general x4, matrix products, attend(): jnp.einsum('hqk,khe->qhe', probs, all_values, preferred_element_type=jnp....  36.6 us
    gather x3, local copies, waits for them, and re-layouts, shards(): jnp.take_along_axis(table, jnp.clip(local_rows, 0, held - 1), axis=1)  35.3 us
    dot_general x1, matrix products, shards(): jnp.dot(expanded, w_down, preferred_element_type=jnp.float32)  28.5 us
  transfers between devices with their start and end apart: 6, of which 6 were waited for; matrix products, arithmetic and copies ran while one was open for 1% of the time, Pallas kernels for 0%

commit v1 on v0

v1 whole, which is shorter than its diff:
```python
import functools

import jax
import jax.numpy as jnp
from jax import lax
from jax.experimental import pallas as pl
from jax.experimental.pallas import tpu as pltpu
from jax.sharding import PartitionSpec as P

D = 1024
HEAD_DIM = 64
KEY_TILE = 256
QUERY_TILE = 256
HEADS_STEP = 4


def layer_norm(values, gain, bias):
    mean = jnp.mean(values, axis=-1, keepdims=True)
    centred = values - mean
    var = jnp.mean(centred * centred, axis=-1, keepdims=True)
    return centred * lax.rsqrt(var + 1e-05) * gain + bias


def attention_kernel(
    bounds_ref, q_ref, k_ref, v_ref, qseg_ref, qgrp_ref, kseg_ref, kgrp_ref, out_ref, *, near
):
    tile = pl.program_id(0)
    first, last = bounds_ref[0, tile], bounds_ref[1, tile]
    q_seg, q_grp = qseg_ref[...], qgrp_ref[...]
    prompt_tiles = (k_ref.shape[1] - near) // KEY_TILE
    tn = (((0,), (0,)), ((), ()))

    def update(start, allowed, state):
        new = []
        for head in range(HEADS_STEP):
            top, total, acc = state[head]
            rows = pl.ds(head * HEAD_DIM, HEAD_DIM)
            logits = lax.dot_general(
                k_ref[rows, pl.ds(start, KEY_TILE)],
                q_ref[rows, :],
                tn,
                preferred_element_type=jnp.float32,
            )
            logits = jnp.where(allowed, logits, -1e30)
            peak = jnp.maximum(top, jnp.max(logits, axis=0, keepdims=True))
            weights = jnp.exp(logits - peak)
            fade = jnp.exp(top - peak)
            total = total * fade + jnp.sum(weights, axis=0, keepdims=True)
            mixed = jnp.dot(
                v_ref[rows, pl.ds(start, KEY_TILE)],
                weights.astype(jnp.bfloat16),
                preferred_element_type=jnp.float32,
            )
            new.append((peak, total, acc * fade + mixed))
        return tuple(new)

    def near_step(number, state):
        start = pl.multiple_of(number * KEY_TILE, KEY_TILE)
        return update(start, kseg_ref[pl.ds(start, KEY_TILE), :] == q_seg, state)

    def prompt_step(number, state):
        start = pl.multiple_of(number * KEY_TILE, KEY_TILE)
        allowed = kgrp_ref[pl.ds(start, KEY_TILE), :] == q_grp
        return update(pl.multiple_of(near + start, KEY_TILE), allowed, state)

    row = (1, QUERY_TILE)
    state = tuple(
        (
            jnp.full(row, -1e30, jnp.float32),
            jnp.zeros(row, jnp.float32),
            jnp.zeros((HEAD_DIM, QUERY_TILE), jnp.float32),
        )
        for _ in range(HEADS_STEP)
    )
    state = lax.fori_loop(first, last, near_step, state)
    state = lax.fori_loop(0, prompt_tiles, prompt_step, state)
    for head in range(HEADS_STEP):
        _, total, acc = state[head]
        out_ref[pl.ds(head * HEAD_DIM, HEAD_DIM), :] = (acc / total).astype(jnp.bfloat16)


def attention(bounds, query, keys, values, q_seg, q_grp, k_seg, k_grp):
    width, rows = query.shape
    every = keys.shape[1]
    near = k_seg.shape[0]
    step = HEADS_STEP * HEAD_DIM
    by_tile = pl.BlockSpec((1, QUERY_TILE), lambda i, j, b: (0, i))
    return pl.pallas_call(
        functools.partial(attention_kernel, near=near),
        out_shape=jax.ShapeDtypeStruct((width, rows), jnp.bfloat16),
        grid_spec=pltpu.PrefetchScalarGridSpec(
            num_scalar_prefetch=1,
            grid=(rows // QUERY_TILE, width // step),
            in_specs=[
                pl.BlockSpec((step, QUERY_TILE), lambda i, j, b: (j, i)),
                pl.BlockSpec((step, every), lambda i, j, b: (j, 0)),
                pl.BlockSpec((step, every), lambda i, j, b: (j, 0)),
                by_tile,
                by_tile,
                pl.BlockSpec((near, 1), lambda i, j, b: (0, 0)),
                pl.BlockSpec((every - near, 1), lambda i, j, b: (0, 0)),
            ],
            out_specs=pl.BlockSpec((step, QUERY_TILE), lambda i, j, b: (j, i)),
        ),
        compiler_params=pltpu.CompilerParams(vmem_limit_bytes=40 << 20),
        cost_estimate=pl.CostEstimate(
            flops=4 * width * rows * 1280, bytes_accessed=8 << 20, transcendentals=16 * rows * 1280
        ),
    )(bounds, query, keys, values, q_seg, q_grp, k_seg, k_grp)


def pick(table, asked):
    texts, held = table.shape
    place = jnp.arange(held, dtype=jnp.int32)
    return jnp.sum(
        jnp.where(asked[:, :, None] == place[None, None, :], table[:, None, :], 0.0), axis=2
    )


def shards(
    tokens,
    prompts,
    w_attn,
    w_out,
    norm_gain,
    norm_bias,
    w_in,
    b_in,
    w_down,
    index_rows,
    lengths,
    groups,
    candidates,
):
    shard_rows = tokens.shape[0]
    parts = lax.axis_size("tensor")
    copies = lax.axis_size("dp")
    me = lax.axis_index("tensor")
    columns = w_attn.shape[2]
    scale = HEAD_DIM ** (-0.5)

    def own_part(weight):
        rows = weight.shape[0] // copies
        return lax.dynamic_slice_in_dim(weight, lax.axis_index("dp") * rows, rows, 0)

    def gather_parts(pieces, width):
        flat = [piece.reshape(-1, width) for piece in pieces]
        got = lax.all_gather(
            jnp.concatenate(flat, axis=0), ("tensor", "dp"), axis=0, tiled=False
        )
        back, at = [], 0
        for piece in flat:
            back.append(got[:, at : at + piece.shape[0]])
            at += piece.shape[0]
        return back

    before = lax.ppermute(tokens, "tensor", [(i, i + 1) for i in range(parts - 1)])
    after = lax.ppermute(tokens, "tensor", [(i + 1, i) for i in range(parts - 1)])
    my_prompts = prompts.reshape(-1, D)
    prompt_rows = my_prompts.shape[0] // parts
    prompt_part = lax.dynamic_slice_in_dim(my_prompts, me * prompt_rows, prompt_rows, 0)
    early = gather_parts(
        [own_part(w_attn.reshape(-1, columns)), own_part(w_out), prompt_part], columns
    )
    attn_all = early[0].reshape(parts, 3, D, columns)
    out_all = early[1].reshape(-1, D)
    flat_prompts = early[2].reshape(parts, copies, -1, D).swapaxes(0, 1).reshape(-1, D)
    late = gather_parts([own_part(w_in), own_part(w_down)], D)
    in_all = late[0].reshape(parts, D, -1)
    down_all = late[1].reshape(-1, D)
    b_all = lax.all_gather(b_in, "tensor", axis=0, tiled=True)

    lens = lengths[0]
    texts_here = lens.shape[0]
    text_ids = jnp.arange(texts_here, dtype=jnp.int32)
    ends = jnp.sum(jnp.where(text_ids[None, :] <= text_ids[:, None], lens[None, :], 0), axis=1)
    near = 3 * shard_rows
    place = jnp.arange(near, dtype=jnp.int32) + (me - 1) * shard_rows
    seg = jnp.sum((place[:, None] >= ends[None, :]).astype(jnp.int32), axis=1)
    k_seg = jnp.where(place >= 0, seg, -1)
    q_seg = seg[shard_rows : 2 * shard_rows]
    q_grp = jnp.sum(jnp.where(q_seg[:, None] == text_ids[None, :], groups[None, :], 0), axis=1)
    k_grp = jnp.arange(flat_prompts.shape[0], dtype=jnp.int32) // prompts.shape[1]
    by_tile = q_seg.reshape(-1, QUERY_TILE)
    least, most = by_tile[:, :1], by_tile[:, -1:]
    first = jnp.sum((k_seg[None, :] < least).astype(jnp.int32), axis=1) // KEY_TILE
    inside = jnp.sum((k_seg[None, :] <= most).astype(jnp.int32), axis=1)
    last = (inside + KEY_TILE - 1) // KEY_TILE
    bounds = jnp.stack([first, last])

    rows = jnp.concatenate([before, tokens, after, flat_prompts], axis=0)

    def project(weight, block):
        return jnp.einsum("tdc,nd->tcn", weight, block, preferred_element_type=jnp.float32)

    query = (project(attn_all[:, 0], tokens) * scale).astype(jnp.bfloat16).reshape(D, -1)
    keys = project(attn_all[:, 1], rows).astype(jnp.bfloat16).reshape(D, -1)
    values = project(attn_all[:, 2], rows).astype(jnp.bfloat16).reshape(D, -1)
    context = attention(
        bounds, query, keys, values, q_seg[None], q_grp[None], k_seg[:, None], k_grp[:, None]
    )
    attended = jnp.einsum("cn,cd->nd", context, out_all, preferred_element_type=jnp.float32)
    normed = layer_norm(
        tokens.astype(jnp.float32) + attended, norm_gain[0], norm_bias[0]
    ).astype(jnp.bfloat16)
    reduced = jnp.zeros((shard_rows, D), jnp.float32)
    units = b_in.shape[0]
    for part in range(parts):
        cols = slice(part * units, (part + 1) * units)
        expanded = jax.nn.gelu(
            jnp.dot(normed, in_all[part], preferred_element_type=jnp.float32) + b_all[cols],
            approximate=False,
        ).astype(jnp.bfloat16)
        reduced += jnp.dot(expanded, down_all[cols], preferred_element_type=jnp.float32)
    output = layer_norm(
        normed.astype(jnp.float32) + reduced, norm_gain[1], norm_bias[1]
    ).astype(jnp.bfloat16)
    member = (text_ids[:, None] == q_seg[None, :]).astype(jnp.bfloat16)
    partial_sums = jnp.dot(member, output, preferred_element_type=jnp.float32)
    pooled_sums = jnp.sum(
        lax.all_to_all(
            partial_sums.reshape(parts, -1, D), "tensor", split_axis=0, concat_axis=0
        ),
        axis=0,
    )
    mine = pooled_sums.shape[0]
    my_lens = lax.dynamic_slice_in_dim(lens, me * mine, mine, 0)
    pooled = pooled_sums / my_lens[:, None].astype(jnp.float32)
    square = jnp.mean(pooled * pooled, axis=1, keepdims=True)
    embedding = (pooled * lax.rsqrt(square + 1e-06)).astype(jnp.bfloat16)
    asked_vectors, asked_rows = (
        lax.all_gather(embedding, "dp", axis=0, tiled=True),
        lax.all_gather(candidates, "dp", axis=0, tiled=True),
    )
    held = index_rows.shape[0]
    local_rows = asked_rows - lax.axis_index("dp") * held
    table = jnp.dot(asked_vectors, index_rows.T, preferred_element_type=jnp.float32) * D ** (-0.5)
    picked = pick(table, local_rows)
    answers = lax.all_to_all(
        picked.astype(jnp.bfloat16).reshape(copies, -1, picked.shape[1]),
        "dp",
        split_axis=0,
        concat_axis=0,
    )
    return jnp.sum(answers.astype(jnp.float32), axis=0)


def solution(mesh):
    placed = (
        P(("dp", "tensor"), None),
        P("dp", None, None),
        P(None, None, "tensor"),
        P("tensor", None),
        P(),
        P(),
        P(None, "tensor"),
        P("tensor"),
        P("tensor", None),
        P("dp", None),
        P("dp", None),
        P("dp"),
        P(("dp", "tensor"), None),
    )
    return jax.shard_map(
        shards, mesh=mesh, in_specs=placed, out_specs=P(("dp", "tensor"), None), check_vma=False
    )
```

time: 693 us -> 316 us (0.46)
  waiting for transfers between devices: 412 us -> 63.5 us
  matrix products: 143 us -> 64.8 us
  Pallas kernels: 0 us -> 53.7 us
  local copies, waits for them, and re-layouts: 61.3 us -> 30.5 us
  blocking collectives: 42 us -> 66.6 us
  starting transfers between devices: 0.43 us -> 10.6 us
    reduce_scatter x3 -> x0, waiting for transfers between devices: 226 us -> none  [the longest x1 142 us: shards(): lax.psum_scatter(jnp.dot(context, w_out, preferred_element_type=jnp.float...]
    all_gather x3 -> x2, waiting for transfers between devices: 184 us -> 57.1 us  [gather_parts(): lax.all_gather(jnp.concatenate(flat, axis=0), ('tensor', 'dp'), axis=0, t...]
    pallas_call x0 -> x1, Pallas kernels: none -> 53.7 us  [attention(): pl.pallas_call(functools.partial(attention_kernel, near=near), out_shape=...]
    sub x4 -> x0, matrix products: 50.9 us -> none  [attend(): weights = jnp.exp(logits - top)]
    all_gather x0 -> x1, blocking collectives: none -> 41.1 us  [shards(): b_all = lax.all_gather(b_in, 'tensor', axis=0, tiled=True)]
    gather x3 -> x0, local copies, waits for them, and re-layouts: 35.3 us -> none  [shards(): jnp.take_along_axis(table, jnp.clip(local_rows, 0, held - 1), axis=1)]
    dot_general x11 -> x8, matrix products: 87.7 us -> 60.1 us  [the longest x4 40.1 us: shards(): jnp.dot(expanded, down_all[cols], preferred_element_type=jnp.float32)]
    unnamed x1 -> x0, blocking collectives: 23.6 us -> none
  transfers between devices with their start and end apart: 6 -> 5, of which waited for: 6 -> 3; matrix products, arithmetic and copies ran while one was open for 1% -> 13% of each run, Pallas kernels for 0% -> 17%
where the time goes in v1:
time: 316 us; the launch traced here: 313 us
  blocking collectives  66.6 us (21%)
  matrix products  64.8 us (21%)
  waiting for transfers between devices  63.5 us (20%)
  Pallas kernels  53.7 us (17%)
  local copies, waits for them, and re-layouts  30.5 us (10%)
  between operations  13.9 us (4%)
  starting transfers between devices  10.6 us (3%)
  other arithmetic  9.04 us (3%)
    all_gather x2, waiting for transfers between devices, gather_parts(): lax.all_gather(jnp.concatenate(flat, axis=0), ('tensor', 'dp'), axis=0, t...  57.1 us
    pallas_call x1, Pallas kernels, attention(): pl.pallas_call(functools.partial(attention_kernel, near=near), out_shape=...  53.7 us
    all_gather x1, blocking collectives, shards(): b_all = lax.all_gather(b_in, 'tensor', axis=0, tiled=True)  41.1 us
    dot_general x4, matrix products, shards(): jnp.dot(expanded, down_all[cols], preferred_element_type=jnp.float32)  40.1 us
    dot_general x3, matrix products, project(): jnp.einsum('tdc,nd->tcn', weight, block, preferred_element_type=jnp.float32)  17.4 us
    slice x1, local copies, waits for them, and re-layouts, shards(): in_all[part]  11.3 us
    slice x3, local copies, waits for them, and re-layouts, gather_parts(): back.append(got[:, at:at + piece.shape[0]])  10.6 us
    all_gather x1, blocking collectives, shards(): lax.all_gather(embedding, 'dp', axis=0, tiled=True)  9.29 us
  transfers between devices with their start and end apart: 5, of which 3 were waited for; matrix products, arithmetic and copies ran while one was open for 13% of the time, Pallas kernels for 17%

profile of v1, /device:TPU:0, one launch (start us, length us, event | category | flops | bytes accessed | tf_op | source)
XLA Modules:
  0.0 312.7 jit_solution(6532917705999274139)
XLA Ops:
  6.5 1.0 constant_dynamic-slice_fusion.4
  7.5 0.1 reshape.279
  7.6 0.0 copy-start.6
  7.6 0.0 copy-start.7
  7.6 0.8 constant_dynamic-slice_fusion.3
  8.4 0.0 copy-done
  8.4 0.0 copy-start.3
  8.4 0.0 copy-start.4
  8.5 0.7 pad_maximum_fusion.1
  9.2 0.0 all-gather.5.cloned.1.call-update
  9.2 0.0 all-gather.7.cloned.1.call-start
  9.3 1.1 constant_dynamic-slice_fusion.1
  10.4 0.8 pad_maximum_fusion
  11.2 0.0 all-gather.7.cloned.1.call-update
  11.2 5.9 %collective-permute-start = (bf16[512,1024]{1,0:T(8,128)(2,1)}, bf16[512,1024]{1,0:T(8,128)(2,1)}, u32[]{:S(2)}, u32[]{:S(2)}) collective-permute-start(bf16[512,1024]{1,0:T(8,128)(2,1)} %param.13), channel_id=1, source_target_pairs={{0,1},{1,2},{2,3},{4,5},{5,6},{6,7},{8,9},{9,10},{10,11},{12,13},{... | collective-permute-start | bytes 3145736 | tf_op jit(solution)/shard_map/ppermute | solution.py:157
  17.1 1.3 collective-permute-start.1
  18.4 0.0 copy-done.8
  18.4 0.1 select_reduce_fusion.2
  18.6 0.1 convert_reduce_fusion
  18.7 0.0 copy-done.5
  18.7 9.1 %all_gather.21 = s32[64,64]{1,0:T(8,128)S(1)} all-gather(s32[8,64]{1,0:T(8,128)S(1)} %copy-done.5), channel_id=1, replica_groups=mesh['dp'=8,'tensor'=4] {'dp'}, dimensions={0}, use_global_device_ids=true | all-gather | bytes 18432 | tf_op jit(solution)/shard_map/all_gather | solution.py:233
  27.8 41.1 %all_gather.26 = f32[4096]{0:T(1024)S(1)} all-gather(f32[1024]{0:T(1024)S(1)} %copy-done.6), channel_id=1, replica_groups=mesh['dp'=8,'tensor'=4] {'tensor'}, dimensions={0}, use_global_device_ids=true | all-gather | bytes 20480 | tf_op jit(solution)/shard_map/all_gather | solution.py:171
  68.8 0.1 fusion.179
  68.9 0.2 slice_reduce_fusion.1
  69.1 0.2 fusion.176
  69.4 0.1 select_reduce_fusion.1
  69.6 0.3 reshape_select_fusion.kseg_ref
  69.8 31.1 %all-gather.5.cloned.1.call-done = bf16[18432,256]{1,0:T(8,128)(2,1)} async-done(((bf16[576,256]{1,0:T(8,128)(2,1)}), bf16[18432,256]{1,0:T(8,128)(2,1)}) %all-gather.5.cloned.1.call-update) | async-done | bytes 9437200 | tf_op jit(solution)/shard_map/all_gather | solution.py:148
  100.9 6.1 %slice.144 = bf16[32,384,256]{2,1,0:T(8,128)(2,1)} slice(bf16[32,576,256]{2,1,0:T(8,128)(2,1)} %bitcast.91), slice={[0:32], [0:384], [0:256]} | slice | bytes 12582912 | tf_op jit(solution)/shard_map/slice | solution.py:153
  107.1 1.3 slice.147
  108.4 3.1 %slice.149 = bf16[32,128,256]{2,1,0:T(8,128)(2,1)} slice(bf16[32,576,256]{2,1,0:T(8,128)(2,1)} %bitcast.93), slice={[0:32], [384:512], [0:256]} | slice | bytes 4194304 | tf_op jit(solution)/shard_map/slice | solution.py:153
  111.5 1.0 reshape.283
  112.6 1.1 copy.31
  113.7 3.1 reshape.287
  116.8 0.0 copy-start.2
  116.8 3.3 %multiply_convert_fusion = bf16[4,256,512]{2,1,0:T(8,128)(2,1)S(1)} fusion(bf16[4,3,1024,256]{3,2,1,0:T(8,128)(2,1)} %bitcast.94, bf16[512,1024]{1,0:T(8,128)(2,1)} %param.13), kind=kOutput, calls=%fused_computation.83 | convolution fusion | flops 1074790400 | bytes 4194304 | tf_op jit(solution)/shard_map/tdc,nd->tcn/dot_general | solution.py:194
  120.1 0.0 collective-permute-done
  120.1 0.0 collective-permute-done.1
  120.1 0.0 copy-done.2
  120.1 7.1 %convolution_convert_fusion.1 = bf16[4,256,2048]{2,1,0:T(8,128)(2,1)S(1)} fusion(bf16[4,3,1024,256]{3,2,1,0:T(8,128)(2,1)} %bitcast.95, bf16[512,1024]{1,0:T(8,128)(2,1)S(1)} %bitcast.106, bf16[512,1024]{1,0:T(8,128)(2,1)} %collective-permute-done.1, bf16[512,1024]{1,0:T(8,128)(2,1)} %param.13, bf16[512,1024]{1,0:T(8,128)(2,1)} %collective-permute-done), kind=kOutput, calls=%fused_computation.4 | convolution fusion | flops 4313841664 | bytes 10485760 | tf_op jit(solution)/shard_map/tdc,nd->tcn/dot_general | solution.py:194
  127.2 7.0 %convolution_convert_fusion = bf16[4,256,2048]{2,1,0:T(8,128)(2,1)S(1)} fusion(bf16[4,3,1024,256]{3,2,1,0:T(8,128)(2,1)} %bitcast.96, bf16[512,1024]{1,0:T(8,128)(2,1)S(1)} %bitcast.107, bf16[512,1024]{1,0:T(8,128)(2,1)} %collective-permute-done.1, bf16[512,1024]{1,0:T(8,128)(2,1)} %param.13, bf16[512,1024]{1,0:T(8,128)(2,1)} %collective-permute-done), kind=kOutput, calls=%fused_computation.3 | convolution fusion | flops 4313841664 | bytes 10485760 | tf_op jit(solution)/shard_map/tdc,nd->tcn/dot_general | solution.py:194
  134.2 53.7 %shard_map.127 = bf16[1024,512]{1,0:T(8,128)(2,1)S(1)} custom-call(s32[2,2]{1,0:T(2,128)S(1)} %pad_add_fusion.bounds_ref, bf16[1024,512]{1,0:T(8,128)(2,1)S(1)} %bitcast.89, bf16[1024,2048]{1,0:T(8,128)(2,1)S(1)} %bitcast.87, bf16[1024,2048]{1,0:T(8,128)(2,1)S(1)} %bitcast.88, s32[1,512]{1,0:T(1,128)S(1)} %bitcast.85, s32[1,512]{1,0:T(1,128)S(1)} %bitcast.86, ...), custom_call_target="tpu_custom_call" | custom-call | flops 2684354560 | bytes 8388608 | tf_op jit(solution)/shard_map/pallas_call | solution.py:88
  188.0 2.6 fusion.306
  190.6 0.4 multiply_reduce_fusion.1
  190.9 0.4 add_convert_fusion.1
  191.3 26.0 %all-gather.7.cloned.1.call-done = bf16[8192,1024]{1,0:T(8,128)(2,1)} async-done(((bf16[256,1024]{1,0:T(8,128)(2,1)}), bf16[8192,1024]{1,0:T(8,128)(2,1)}) %all-gather.7.cloned.1.call-update) | async-done | bytes 16777232 | tf_op jit(solution)/shard_map/all_gather | solution.py:148
  217.3 11.3 %fusion.302 = (bf16[8,128,1024]{2,1,0:T(8,128)(2,1)}, bf16[8,128,1024]{2,1,0:T(8,128)(2,1)}, bf16[8,128,1024]{2,1,0:T(8,128)(2,1)S(1)}, bf16[8,128,1024]{2,1,0:T...) fusion(bf16[32,256,1024]{2,1,0:T(8,128)(2,1)} %bitcast.90), kind=kLoop, calls=%fused_computation.403 | loop fusion | bytes 33554432 | tf_op jit(solution)/shard_map/slice | solution.py:211
  228.6 9.9 %fusion.42 = f32[512,1024]{1,0:T(8,128)} fusion(bf16[1024,1024]{1,0:T(8,128)(2,1)} %bitcast.104, bf16[512,1024]{1,0:T(8,128)(2,1)S(1)} %add_convert_fusion.1, bf16[1024,1024]{1,0:T(8,128)(2,1)} %bitcast.105, f32[1024]{0:T(1024)S(1)} %get-tuple-element.19), kind=kOutput, calls=%fused_computation.94 | convolution fusion | flops 2182086656 | bytes 7344128 | tf_op jit(solution)/shard_map/dot_general | solution.py:214
  238.5 9.8 %fusion.43 = f32[512,1024]{1,0:T(8,128)} fusion(bf16[1024,1024]{1,0:T(8,128)(2,1)} %bitcast.102, bf16[512,1024]{1,0:T(8,128)(2,1)S(1)} %add_convert_fusion.1, bf16[1024,1024]{1,0:T(8,128)(2,1)} %bitcast.103, f32[1024]{0:T(1024)S(1)} %get-tuple-element.20), kind=kOutput, calls=%fused_computation.95 | convolution fusion | flops 2182086656 | bytes 7344128 | tf_op jit(solution)/shard_map/dot_general | solution.py:214
  248.3 9.6 %fusion.41 = f32[512,1024]{1,0:T(8,128)} fusion(bf16[1024,1024]{1,0:T(8,128)(2,1)S(1)} %bitcast.100, bf16[512,1024]{1,0:T(8,128)(2,1)S(1)} %add_convert_fusion.1, bf16[1024,1024]{1,0:T(8,128)(2,1)} %bitcast.101, f32[1024]{0:T(1024)S(1)} %get-tuple-element.18), kind=kOutput, calls=%fused_computation.93 | convolution fusion | flops 2182086656 | bytes 7344128 | tf_op jit(solution)/shard_map/dot_general | solution.py:214
  258.0 10.8 %fusion.307 = (f32[512]{0:T(512)S(1)}, f32[512,1024]{1,0:T(8,128)S(1)}) fusion(bf16[1024,1024]{1,0:T(8,128)(2,1)} %bitcast.99, bf16[512,1024]{1,0:T(8,128)(2,1)S(1)} %add_convert_fusion.1, bf16[1024,1024]{1,0:T(8,128)(2,1)} %bitcast.98, f32[1024]{0:T(1024)S(1)} %get-tuple-element.17, f32[512,1024]{1,0:T(8,128)} %fusion.41, f32[512,1024]{1,0:T(8,128)} %fusion.43, ...), kind=kOutput, calls=%fused_computation.408 | convolution fusion | flops 2185231872 | bytes 13637632 | tf_op jit(solution)/shard_map/dot_general | solution.py:214
  268.8 0.3 multiply_reduce_fusion
  269.1 1.2 convolution_bitcast_fusion
  270.3 3.3 %all-to-all-start = ((f32[4,8,1024]{2,1,0:T(8,128)}), f32[4,8,1024]{2,1,0:T(8,128)S(1)}, u32[]{:S(2)}, u32[]{:S(2)}) async-start(f32[4,8,1024]{2,1,0:T(8,128)} %convolution_bitcast_fusion), calls=%async_computation | async-start | bytes 262144 | tf_op jit(solution)/shard_map/all_to_all | solution.py:221
  273.7 6.4 %all-to-all-done = f32[4,8,1024]{2,1,0:T(8,128)S(1)} async-done(((f32[4,8,1024]{2,1,0:T(8,128)}), f32[4,8,1024]{2,1,0:T(8,128)S(1)}, u32[]{:S(2)}, u32[]{:S(2)}) %all-to-all-start) | async-done | bytes 131104 | tf_op jit(solution)/shard_map/all_to_all | solution.py:221
  280.0 0.2 multiply_reduce_fusion.2
  280.2 0.1 multiply_convert_fusion.1
  280.3 9.3 %all_gather.27 = bf16[64,1024]{1,0:T(8,128)(2,1)S(1)} all-gather(bf16[8,1024]{1,0:T(8,128)(2,1)S(1)} %multiply_convert_fusion.1), channel_id=1, replica_groups=mesh['dp'=8,'tensor'=4] {'dp'}, dimensions={0}, use_global_device_ids=true | all-gather | bytes 147456 | tf_op jit(solution)/shard_map/all_gather | solution.py:232
  289.6 3.6 %convolution_multiply_fusion = f32[64,2048]{1,0:T(8,128)S(1)} fusion(bf16[64,1024]{1,0:T(8,128)(2,1)S(1)} %all_gather.27, bf16[2048,1024]{1,0:T(8,128)(2,1)} %param.22), kind=kOutput, calls=%fused_computation.9 | convolution fusion | flops 268566528 | bytes 4849664 | tf_op jit(solution)/shard_map/dot_general | solution.py:237
  293.2 4.5 %select_reduce_fusion = bf16[64,64]{1,0:T(8,128)(2,1)S(1)} fusion(f32[64,2048]{1,0:T(8,128)S(1)} %convolution_multiply_fusion, s32[64,64]{1,0:T(8,128)S(1)} %broadcast_subtract_fusion), kind=kLoop, calls=%fused_computation | loop fusion | flops 25161728 | bytes 548864 | tf_op jit(solution)/shard_map/reduce_sum | solution.py:115
  297.7 0.1 reshape.295
  297.8 7.2 %all_to_all.10 = bf16[8,2,256]{2,1,0:T(2,128)(2,1)S(1)} all-to-all(bf16[8,2,256]{2,1,0:T(2,128)(2,1)S(1)} %reshape.295), channel_id=1, replica_groups=mesh['dp'=8,'tensor'=4] {'dp'}, dimensions={0} | all-to-all | bytes 16384 | tf_op jit(solution)/shard_map/all_to_all | solution.py:239
  305.0 0.1 reshape.296
  305.1 0.6 convert_reduce_fusion.1
  (29 shorter events, 0.2 us)
Async XLA Ops:
  6.5 1.9 copy-start
  6.5 94.4 %all-gather.5.cloned.1.call-start = ((), (), s32[]{:S(2)}) async-start(), calls=%async_computation.2 | async-start | bytes 9732096 | tf_op jit(solution)/shard_map/all_gather | solution.py:148
  7.5 10.9 %copy-start.8 = (s32[1,32]{1,0:T(1,128)S(1)}, s32[1,32]{1,0:T(1,128)}, u32[]{:S(2)}) copy-start(s32[1,32]{1,0:T(1,128)} %param.23) | copy-start | bytes 388
  7.5 11.2 %copy-start.5 = (s32[8,64]{1,0:T(8,128)S(1)}, s32[8,64]{1,0:T(8,128)}, u32[]{:S(2)}) copy-start(s32[8,64]{1,0:T(8,128)} %param.25) | copy-start | bytes 6148
  7.6 20.2 %copy-start.6 = (f32[1024]{0:T(1024)S(1)}, f32[1024]{0:T(1024)}, u32[]{:S(2)}) copy-start(f32[1024]{0:T(1024)} %param.20) | copy-start | bytes 12292
  7.6 61.8 %copy-start.7 = (s32[32]{0:T(128)S(1)}, s32[32]{0:T(128)}, u32[]{:S(2)}) copy-start(s32[32]{0:T(128)} %param.24) | copy-start | bytes 388
  8.4 61.1 %copy-start.3 = (f32[2,1024]{1,0:T(2,128)S(1)}, f32[2,1024]{1,0:T(2,128)}, u32[]{:S(2)}) copy-start(f32[2,1024]{1,0:T(2,128)} %param.17) | copy-start | bytes 24580
  8.4 61.1 %copy-start.4 = (f32[2,1024]{1,0:T(2,128)S(1)}, f32[2,1024]{1,0:T(2,128)}, u32[]{:S(2)}) copy-start(f32[2,1024]{1,0:T(2,128)} %param.18) | copy-start | bytes 24580
  9.2 208.1 %all-gather.7.cloned.1.call-start = ((), (), s32[]{:S(2)}) async-start(), calls=%async_computation.3 | async-start | bytes 17301504 | tf_op jit(solution)/shard_map/all_gather | solution.py:148
  11.2 108.9 %collective-permute-start = (bf16[512,1024]{1,0:T(8,128)(2,1)}, bf16[512,1024]{1,0:T(8,128)(2,1)}, u32[]{:S(2)}, u32[]{:S(2)}) collective-permute-start(bf16[512,1024]{1,0:T(8,128)(2,1)} %param.13), channel_id=1, source_target_pairs={{0,1},{1,2},{2,3},{4,5},{5,6},{6,7},{8,9},{9,10},{10,11},{12,13},{... | collective-permute-start | bytes 3145736 | tf_op jit(solution)/shard_map/ppermute | solution.py:157
  17.1 103.0 %collective-permute-start.1 = (bf16[512,1024]{1,0:T(8,128)(2,1)}, bf16[512,1024]{1,0:T(8,128)(2,1)}, u32[]{:S(2)}, u32[]{:S(2)}) collective-permute-start(bf16[512,1024]{1,0:T(8,128)(2,1)} %param.13), channel_id=1, source_target_pairs={{1,0},{2,1},{3,2},{5,4},{6,5},{7,6},{9,8},{10,9},{11,10},{13,12},{... | collective-permute-start | bytes 3145736 | tf_op jit(solution)/shard_map/ppermute | solution.py:158
  116.8 3.3 %copy-start.2 = (bf16[8,4,16,1024]{3,2,1,0:T(8,128)(2,1)S(1)}, bf16[8,4,16,1024]{3,2,1,0:T(8,128)(2,1)}, u32[]{:S(2)}) copy-start(bf16[8,4,16,1024]{3,2,1,0:T(8,128)(2,1)} %copy.31) | copy-start | bytes 3145732
  270.3 9.7 %all-to-all-start = ((f32[4,8,1024]{2,1,0:T(8,128)}), f32[4,8,1024]{2,1,0:T(8,128)S(1)}, u32[]{:S(2)}, u32[]{:S(2)}) async-start(f32[4,8,1024]{2,1,0:T(8,128)} %convolution_bitcast_fusion), calls=%async_computation | async-start | bytes 262144 | tf_op jit(solution)/shard_map/all_to_all | solution.py:221
  280.3 25.4 %copy-start.1 = (bf16[3,1024,256]{2,1,0:T(8,128)(2,1)S(1)}, bf16[3,1024,256]{2,1,0:T(8,128)(2,1)}, u32[]{:S(2)}) copy-start(bf16[3,1024,256]{2,1,0:T(8,128)(2,1)} %param.15) | copy-start | bytes 4718596
Sparse Core Ops, SparseCore 0:
  10.3 90.6 all-gather.4
  103.8 113.4 all-gather.6
